TPU v7x, 256 devices: a whole 4x4x8 slice. The times are simulated.
256 devices in a mesh: pipe: 16 (over x, y), expert: 16 (over z, core).
Axes of the slice: x: 4, y: 4, z: 8, core: 2. Of those that a mesh axis runs over, the one named last changes fastest.
Arguments:
- fwd_acts: bfloat16 [16, 1024, 3584], P('pipe', 'expert'), may hold values from -6 to 6
- fwd_route: int32 [16, 1024, 1], P('pipe', 'expert'), may hold values from 0 to 3; in each aligned block of 64 rows (0 to 63, 64 to 127, ..., all dimensions but the last counted through in order) at most 24 rows name the same one
- fwd_gate: float32 [16, 1024, 1], P('pipe', 'expert'), may hold values from 0.1 to 1
- saved_x: bfloat16 [16, 1024, 3584], P('pipe', 'expert'), may hold values from -6 to 6
- bwd_grads: bfloat16 [16, 1024, 3584], P('pipe', 'expert'), may hold values from -6 to 6
- bwd_route: int32 [16, 1024, 1], P('pipe', 'expert'), may hold values from 0 to 3; in each aligned block of 64 rows (0 to 63, 64 to 127, ..., all dimensions but the last counted through in order) at most 24 rows name the same one
- bwd_gate: float32 [16, 1024, 1], P('pipe', 'expert'), may hold values from 0.1 to 1
- w_gate: bfloat16 [16, 3584, 8192], P('pipe', None, 'expert'), may hold values from -0.09375 to 0.09375
- w_up: bfloat16 [16, 3584, 8192], P('pipe', None, 'expert'), may hold values from -0.09375 to 0.09375
- w_down: bfloat16 [16, 8192, 3584], P('pipe', 'expert'), may hold values from -0.125 to 0.125
Outputs:
- fwd_out: bfloat16 [16, 1024, 3584], P('pipe', 'expert')
- grad_out: bfloat16 [16, 1024, 3584], P('pipe', 'expert')
Inputs may be any that keep to these rules, and one draw needn't show every extreme that they name: `fwd_route`: in each aligned block of 64 rows (the rows of one device) no expert is named by more than 24 rows, a bound that some block reaches. `bwd_route`: in each aligned block of 64 rows (the rows of one device) no expert is named by more than 24 rows, a bound that some block reaches.
All inputs are finite; a program needn't handle non-finite values.
Results may differ from a plain program's by a relative error of at most 0.0039.
Values may be sent and summed in bfloat16 or wider, within the bound.
A program may use at most 128 MiB of HBM per device.

v0:
```python
import jax
import jax.numpy as jnp
from jax import lax
from jax.sharding import PartitionSpec as P

EXP_SECTION = 4
MOST = 24


def passed_along(block, axis, distance):
    devices = range(lax.axis_size(axis))
    route = [((i - distance) % len(devices), i) for i in devices]
    return lax.ppermute(block, axis, route)


def slot_maps(route, gates):
    experts_hot = (
        route[:, :, None] == jnp.arange(EXP_SECTION, dtype=jnp.int32)[None, None, :]
    ).astype(jnp.int32)
    per_token = jnp.sum(experts_hot, axis=1)
    before = jnp.cumsum(per_token, axis=0) - per_token
    ranked = jnp.sum(experts_hot * before[:, None, :], axis=2)
    slots_hot = (ranked[:, :, None] == jnp.arange(MOST, dtype=jnp.int32)[None, None, :]).astype(
        jnp.float32
    )
    expert_float = experts_hot.astype(jnp.float32)
    placing = jnp.einsum(
        "tke,tkm->emt", expert_float, slots_hot, precision=lax.Precision.HIGHEST
    ).astype(jnp.bfloat16)
    mixing = jnp.einsum(
        "tke,tkm,tk->tem", expert_float, slots_hot, gates, precision=lax.Precision.HIGHEST
    )
    return (placing, mixing)


def pack_rows(placing, tokens, split_count):
    buffer = jnp.einsum("emt,td->emd", placing, tokens, preferred_element_type=jnp.float32).astype(
        jnp.bfloat16
    )
    return jnp.repeat(buffer, split_count, axis=0)


def unpack_rows(returned, mixing, split_count):
    sources, slot_count, features = returned.shape
    combined = (
        returned.astype(jnp.float32)
        .reshape(EXP_SECTION, split_count, slot_count, features)
        .sum(axis=1)
    )
    return jnp.einsum("tem,emd->td", mixing, combined, precision=lax.Precision.HIGHEST)


def expert_forward(received, gate_weight, up_weight, down_weight):
    sources, slot_count, features = received.shape
    token_rows = received.reshape(sources * slot_count, features)
    gate_pre = jnp.dot(token_rows, gate_weight, preferred_element_type=jnp.float32)
    up_pre = jnp.dot(token_rows, up_weight, preferred_element_type=jnp.float32)
    active = (jax.nn.silu(gate_pre) * up_pre).astype(jnp.bfloat16)
    output = jnp.dot(active, down_weight, preferred_element_type=jnp.float32).astype(jnp.bfloat16)
    return output.reshape(sources, slot_count, features)


def expert_backward(received_x, received_g, gate_weight, up_weight, down_weight):
    sources, slot_count, features = received_x.shape
    contract = (((1,), (1,)), ((), ()))
    token_rows = received_x.reshape(sources * slot_count, features)
    grad_rows = received_g.reshape(sources * slot_count, features)
    gate_pre = jnp.dot(token_rows, gate_weight, preferred_element_type=jnp.float32)
    up_pre = jnp.dot(token_rows, up_weight, preferred_element_type=jnp.float32)
    sigmoid_gate = jax.nn.sigmoid(gate_pre)
    hidden_grad = lax.dot_general(
        grad_rows, down_weight, contract, preferred_element_type=jnp.float32
    )
    grad_up = (hidden_grad * gate_pre * sigmoid_gate).astype(jnp.bfloat16)
    grad_gate = (
        hidden_grad * up_pre * sigmoid_gate * (1.0 + gate_pre * (1.0 - sigmoid_gate))
    ).astype(jnp.bfloat16)
    output = lax.dot_general(grad_gate, gate_weight, contract, preferred_element_type=jnp.float32)
    output = output + lax.dot_general(
        grad_up, up_weight, contract, preferred_element_type=jnp.float32
    )
    return output.astype(jnp.bfloat16).reshape(sources, slot_count, features)


def local(
    fwd_acts, fwd_route, fwd_gate, saved_x, bwd_grads, bwd_route, bwd_gate, w_gate, w_up, w_down
):
    split_count = lax.axis_size("expert") // EXP_SECTION
    inputs = passed_along(fwd_acts[0], "pipe", 1)
    upstream = passed_along(bwd_grads[0], "pipe", -1)
    gate_weight = w_gate[0]
    up_weight = w_up[0]
    down_weight = w_down[0]
    fwd_place, fwd_mix = slot_maps(fwd_route[0], fwd_gate[0])
    bwd_place, bwd_mix = slot_maps(bwd_route[0], bwd_gate[0])
    fwd_send = pack_rows(fwd_place, inputs, split_count)
    saved_send = pack_rows(bwd_place, saved_x[0], split_count)
    grad_send = pack_rows(bwd_place, upstream, split_count)
    forward_part = expert_forward(
        lax.all_to_all(fwd_send, "expert", split_axis=0, concat_axis=0, tiled=True),
        gate_weight,
        up_weight,
        down_weight,
    )
    fwd_back = lax.all_to_all(forward_part, "expert", split_axis=0, concat_axis=0, tiled=True)
    backward_part = expert_backward(
        lax.all_to_all(saved_send, "expert", split_axis=0, concat_axis=0, tiled=True),
        lax.all_to_all(grad_send, "expert", split_axis=0, concat_axis=0, tiled=True),
        gate_weight,
        up_weight,
        down_weight,
    )
    bwd_back = lax.all_to_all(backward_part, "expert", split_axis=0, concat_axis=0, tiled=True)
    fwd_out = (inputs.astype(jnp.float32) + unpack_rows(fwd_back, fwd_mix, split_count)).astype(
        jnp.bfloat16
    )
    grad_out = (upstream.astype(jnp.float32) + unpack_rows(bwd_back, bwd_mix, split_count)).astype(
        jnp.bfloat16
    )
    return (fwd_out[None], grad_out[None])


def solution(mesh):
    placed = (
        P("pipe", "expert", None),
        P("pipe", "expert", None),
        P("pipe", "expert", None),
        P("pipe", "expert", None),
        P("pipe", "expert", None),
        P("pipe", "expert", None),
        P("pipe", "expert", None),
        P("pipe", None, "expert"),
        P("pipe", None, "expert"),
        P("pipe", "expert", None),
    )
    return jax.shard_map(
        local,
        mesh=mesh,
        in_specs=placed,
        out_specs=(P("pipe", "expert", None), P("pipe", "expert", None)),
        check_vma=False,
    )
```

profile of v0, /device:TPU:97, one launch (start us, length us, event | category | flops | bytes accessed | tf_op | source)
XLA Modules:
  0.0 360.8 jit_solution(11094548043930716010)
XLA Ops:
  0.6 2.2 fusion.83
  3.9 1.7 broadcast_in_dim.26
  5.6 8.0 %all-to-all-start.3 = ((bf16[16,24,3584]{2,1,0:T(8,128)(2,1)}), bf16[16,24,3584]{2,1,0:T(8,128)(2,1)S(1)}, u32[]{:S(2)}, u32[]{:S(2)}) async-start(bf16[16,24,3584]{2,1,0:T(8,128)(2,1)} %bitcast.23), calls=%async_computation.3 | async-start | bytes 5505024 | tf_op jit(solution)/shard_map/all_to_all | solution.py:107
  13.6 4.9 %collective-permute-start.1 = (bf16[64,3584]{1,0:T(8,128)(2,1)}, bf16[64,3584]{1,0:T(8,128)(2,1)S(1)}, u32[]{:S(2)}, u32[]{:S(2)}) collective-permute-start(bf16[64,3584]{1,0:T(8,128)(2,1)} %bitcast.100), channel_id=1, source_target_pairs={{16,0},{32,16},{48,32},{64,48},{80,64},{96,80},{112,96},{128,112},... | collective-permute-start | bytes 1376264 | tf_op jit(solution)/shard_map/ppermute | solution.py:13
  18.6 9.9 %collective-permute-done.1 = bf16[64,3584]{1,0:T(8,128)(2,1)S(1)} collective-permute-done((bf16[64,3584]{1,0:T(8,128)(2,1)}, bf16[64,3584]{1,0:T(8,128)(2,1)S(1)}, u32[]{:S(2)}, u32[]{:S(2)}) %collective-permute-start.1) | collective-permute-done | bytes 458784 | tf_op jit(solution)/shard_map/ppermute | solution.py:13
  29.2 1.2 convolution_convert_fusion.2
  30.4 46.0 %all-to-all-done.3 = bf16[16,24,3584]{2,1,0:T(8,128)(2,1)S(1)} async-done(((bf16[16,24,3584]{2,1,0:T(8,128)(2,1)}), bf16[16,24,3584]{2,1,0:T(8,128)(2,1)S(1)}, u32[]{:S(2)}, u32[]{:S(2)}) %all-to-all-start.3) | async-done | bytes 2752544 | tf_op jit(solution)/shard_map/all_to_all | solution.py:107
  76.3 2.9 broadcast_in_dim.12
  79.2 5.4 %all-to-all-start.2 = ((bf16[16,24,3584]{2,1,0:T(8,128)(2,1)}), bf16[16,24,3584]{2,1,0:T(8,128)(2,1)}, u32[]{:S(2)}, u32[]{:S(2)}) async-start(bf16[16,24,3584]{2,1,0:T(8,128)(2,1)} %bitcast.19), calls=%async_computation.2 | async-start | bytes 5505024 | tf_op jit(solution)/shard_map/all_to_all | solution.py:108
  84.6 1.3 collective-permute-start
  85.9 1.4 fusion.82
  87.4 12.8 %collective-permute-done = bf16[64,3584]{1,0:T(8,128)(2,1)S(1)} collective-permute-done((bf16[64,3584]{1,0:T(8,128)(2,1)}, bf16[64,3584]{1,0:T(8,128)(2,1)S(1)}, u32[]{:S(2)}, u32[]{:S(2)}) %collective-permute-start) | collective-permute-done | bytes 458784 | tf_op jit(solution)/shard_map/ppermute | solution.py:13
  100.2 0.8 copy-done.4
  101.0 1.2 convolution_convert_fusion.3
  102.2 45.3 %all-to-all-done.2 = bf16[16,24,3584]{2,1,0:T(8,128)(2,1)} async-done(((bf16[16,24,3584]{2,1,0:T(8,128)(2,1)}), bf16[16,24,3584]{2,1,0:T(8,128)(2,1)}, u32[]{:S(2)}, u32[]{:S(2)}) %all-to-all-start.2) | async-done | bytes 2752544 | tf_op jit(solution)/shard_map/all_to_all | solution.py:108
  147.5 2.9 broadcast_in_dim.10
  150.4 5.3 %all-to-all-start = ((bf16[16,24,3584]{2,1,0:T(8,128)(2,1)}), bf16[16,24,3584]{2,1,0:T(8,128)(2,1)}, u32[]{:S(2)}, u32[]{:S(2)}) async-start(bf16[16,24,3584]{2,1,0:T(8,128)(2,1)} %bitcast.5), calls=%async_computation | async-start | bytes 5505024 | tf_op jit(solution)/shard_map/all_to_all | solution.py:100
  155.7 4.7 %fusion.11 = f32[384,512]{1,0:T(8,128)} fusion(bf16[384,3584]{1,0:T(8,128)(2,1)S(1)} %bitcast.91, bf16[1,3584,512]{2,1,0:T(8,128)(2,1)} %param.17), kind=kOutput, calls=%fused_computation.20 | convolution fusion | flops 1409286144 | bytes 7208960 | tf_op jit(solution)/shard_map/dot_general | solution.py:68
  160.3 4.3 %fusion.1 = f32[384,512]{1,0:T(8,128)} fusion(bf16[384,3584]{1,0:T(8,128)(2,1)} %bitcast.20, bf16[1,512,3584]{2,1,0:T(8,128)(2,1)S(1)} %copy-done.9), kind=kOutput, calls=%fused_computation.10 | convolution fusion | flops 1409286144 | bytes 7208960 | tf_op jit(solution)/shard_map/dot_general | solution.py:71
  164.6 9.2 %fusion.9 = f32[384,3584]{1,0:T(8,128)} fusion(bf16[1,3584,512]{2,1,0:T(8,128)(2,1)} %param.17, f32[384,512]{1,0:T(8,128)} %fusion.1, bf16[384,3584]{1,0:T(8,128)(2,1)S(1)} %bitcast.92, bf16[1,3584,512]{2,1,0:T(8,128)(2,1)} %param.18, f32[384,512]{1,0:T(8,128)} %fusion.11), kind=kOutput, calls=%fused_computation.18 | convolution fusion | flops 2820538368 | bytes 17170432 | tf_op jit(solution)/shard_map/dot_general | solution.py:78
  173.8 7.4 %fusion = bf16[384,3584]{1,0:T(8,128)(2,1)} fusion(f32[384,3584]{1,0:T(8,128)} %fusion.9, bf16[1,3584,512]{2,1,0:T(8,128)(2,1)} %param.18, f32[384,512]{1,0:T(8,128)} %fusion.1, f32[384,512]{1,0:T(8,128)} %fusion.11), kind=kOutput, calls=%fused_computation.1 | convolution fusion | flops 1413218304 | bytes 13500416 | tf_op jit(solution)/shard_map/dot_general | solution.py:79
  181.3 37.2 %all-to-all-done = bf16[16,24,3584]{2,1,0:T(8,128)(2,1)} async-done(((bf16[16,24,3584]{2,1,0:T(8,128)(2,1)}), bf16[16,24,3584]{2,1,0:T(8,128)(2,1)}, u32[]{:S(2)}, u32[]{:S(2)}) %all-to-all-start) | async-done | bytes 2752544 | tf_op jit(solution)/shard_map/all_to_all | solution.py:100
  218.5 5.3 %all-to-all-start.4 = ((bf16[16,24,3584]{2,1,0:T(8,128)(2,1)}), bf16[16,24,3584]{2,1,0:T(8,128)(2,1)S(1)}, u32[]{:S(2)}, u32[]{:S(2)}) async-start(bf16[16,24,3584]{2,1,0:T(8,128)(2,1)} %bitcast.25), calls=%async_computation.4 | async-start | bytes 5505024 | tf_op jit(solution)/shard_map/all_to_all | solution.py:113
  223.8 5.3 %fusion.13 = f32[384,512]{1,0:T(8,128)} fusion(bf16[384,3584]{1,0:T(8,128)(2,1)} %bitcast.6, bf16[1,3584,512]{2,1,0:T(8,128)(2,1)} %param.17), kind=kOutput, calls=%fused_computation.22 | convolution fusion | flops 1409286144 | bytes 7208960 | tf_op jit(solution)/shard_map/dot_general | solution.py:56
  229.1 8.9 %convolution_convert_fusion = bf16[384,3584]{1,0:T(8,128)(2,1)} fusion(bf16[1,512,3584]{2,1,0:T(8,128)(2,1)} %param.19, bf16[384,3584]{1,0:T(8,128)(2,1)} %bitcast.6, bf16[1,3584,512]{2,1,0:T(8,128)(2,1)} %param.18, f32[384,512]{1,0:T(8,128)} %fusion.13), kind=kOutput, calls=%fused_computation.2 | convolution fusion | flops 2821128192 | bytes 13631488 | tf_op jit(solution)/shard_map/dot_general | solution.py:59
  238.0 48.5 %all-to-all-done.4 = bf16[16,24,3584]{2,1,0:T(8,128)(2,1)S(1)} async-done(((bf16[16,24,3584]{2,1,0:T(8,128)(2,1)}), bf16[16,24,3584]{2,1,0:T(8,128)(2,1)S(1)}, u32[]{:S(2)}, u32[]{:S(2)}) %all-to-all-start.4) | async-done | bytes 2752544 | tf_op jit(solution)/shard_map/all_to_all | solution.py:113
  286.5 5.4 %all-to-all-start.1 = ((bf16[16,24,3584]{2,1,0:T(8,128)(2,1)}), bf16[16,24,3584]{2,1,0:T(8,128)(2,1)}, u32[]{:S(2)}, u32[]{:S(2)}) async-start(bf16[16,24,3584]{2,1,0:T(8,128)(2,1)} %bitcast.93), calls=%async_computation.1 | async-start | bytes 5505024 | tf_op jit(solution)/shard_map/all_to_all | solution.py:105
  291.9 1.5 convert_reduce_fusion
  293.4 61.3 %all-to-all-done.1 = bf16[16,24,3584]{2,1,0:T(8,128)(2,1)} async-done(((bf16[16,24,3584]{2,1,0:T(8,128)(2,1)}), bf16[16,24,3584]{2,1,0:T(8,128)(2,1)}, u32[]{:S(2)}, u32[]{:S(2)}) %all-to-all-start.1) | async-done | bytes 2752544 | tf_op jit(solution)/shard_map/all_to_all | solution.py:105
  354.7 2.4 convert_reduce_fusion.1
  357.1 1.8 fusion.43
  359.0 1.8 fusion.42
  (26 shorter events, 1.8 us)
Async XLA Ops:
  0.6 2.9 copy-start
  5.6 70.7 %all-to-all-start.3 = ((bf16[16,24,3584]{2,1,0:T(8,128)(2,1)}), bf16[16,24,3584]{2,1,0:T(8,128)(2,1)S(1)}, u32[]{:S(2)}, u32[]{:S(2)}) async-start(bf16[16,24,3584]{2,1,0:T(8,128)(2,1)} %bitcast.23), calls=%async_computation.3 | async-start | bytes 5505024 | tf_op jit(solution)/shard_map/all_to_all | solution.py:107
  13.6 14.8 %collective-permute-start.1 = (bf16[64,3584]{1,0:T(8,128)(2,1)}, bf16[64,3584]{1,0:T(8,128)(2,1)S(1)}, u32[]{:S(2)}, u32[]{:S(2)}) collective-permute-start(bf16[64,3584]{1,0:T(8,128)(2,1)} %bitcast.100), channel_id=1, source_target_pairs={{16,0},{32,16},{48,32},{64,48},{80,64},{96,80},{112,96},{128,112},... | collective-permute-start | bytes 1376264 | tf_op jit(solution)/shard_map/ppermute | solution.py:13
  28.4 0.8 copy-start.2
  79.2 6.7 %copy-start.6 = (s32[1,64,1]{1,2,0:T(1,128)S(1)}, s32[1,64,1]{1,2,0:T(1,128)}, u32[]{:S(2)}) copy-start(s32[1,64,1]{1,2,0:T(1,128)} %param.11) | copy-start | bytes 772
  79.2 68.2 %all-to-all-start.2 = ((bf16[16,24,3584]{2,1,0:T(8,128)(2,1)}), bf16[16,24,3584]{2,1,0:T(8,128)(2,1)}, u32[]{:S(2)}, u32[]{:S(2)}) async-start(bf16[16,24,3584]{2,1,0:T(8,128)(2,1)} %bitcast.19), calls=%async_computation.2 | async-start | bytes 5505024 | tf_op jit(solution)/shard_map/all_to_all | solution.py:108
  84.6 15.6 %collective-permute-start = (bf16[64,3584]{1,0:T(8,128)(2,1)}, bf16[64,3584]{1,0:T(8,128)(2,1)S(1)}, u32[]{:S(2)}, u32[]{:S(2)}) collective-permute-start(bf16[64,3584]{1,0:T(8,128)(2,1)} %bitcast.101), channel_id=1, source_target_pairs={{240,0},{0,16},{16,32},{32,48},{48,64},{64,80},{80,96},{96,112},{1... | collective-permute-start | bytes 1376264 | tf_op jit(solution)/shard_map/ppermute | solution.py:13
  100.2 0.8 copy-start.4
  150.4 68.1 %all-to-all-start = ((bf16[16,24,3584]{2,1,0:T(8,128)(2,1)}), bf16[16,24,3584]{2,1,0:T(8,128)(2,1)}, u32[]{:S(2)}, u32[]{:S(2)}) async-start(bf16[16,24,3584]{2,1,0:T(8,128)(2,1)} %bitcast.5), calls=%async_computation | async-start | bytes 5505024 | tf_op jit(solution)/shard_map/all_to_all | solution.py:100
  155.7 4.7 %copy-start.9 = (bf16[1,512,3584]{2,1,0:T(8,128)(2,1)S(1)}, bf16[1,512,3584]{2,1,0:T(8,128)(2,1)}, u32[]{:S(2)}) copy-start(bf16[1,512,3584]{2,1,0:T(8,128)(2,1)} %param.19) | copy-start | bytes 11010052
  218.5 68.0 %all-to-all-start.4 = ((bf16[16,24,3584]{2,1,0:T(8,128)(2,1)}), bf16[16,24,3584]{2,1,0:T(8,128)(2,1)S(1)}, u32[]{:S(2)}, u32[]{:S(2)}) async-start(bf16[16,24,3584]{2,1,0:T(8,128)(2,1)} %bitcast.25), calls=%async_computation.4 | async-start | bytes 5505024 | tf_op jit(solution)/shard_map/all_to_all | solution.py:113
  286.5 5.4 %copy-start.7 = (f32[1,64,1]{1,2,0:T(1,128)S(1)}, f32[1,64,1]{1,2,0:T(1,128)}, u32[]{:S(2)}) copy-start(f32[1,64,1]{1,2,0:T(1,128)} %param.16) | copy-start | bytes 772
  286.5 5.4 %copy-start.8 = (f32[1,64,1]{1,2,0:T(1,128)S(1)}, f32[1,64,1]{1,2,0:T(1,128)}, u32[]{:S(2)}) copy-start(f32[1,64,1]{1,2,0:T(1,128)} %param.12) | copy-start | bytes 772
  286.5 68.2 %all-to-all-start.1 = ((bf16[16,24,3584]{2,1,0:T(8,128)(2,1)}), bf16[16,24,3584]{2,1,0:T(8,128)(2,1)}, u32[]{:S(2)}, u32[]{:S(2)}) async-start(bf16[16,24,3584]{2,1,0:T(8,128)(2,1)} %bitcast.93), calls=%async_computation.1 | async-start | bytes 5505024 | tf_op jit(solution)/shard_map/all_to_all | solution.py:105
  293.4 63.7 %copy-start.1 = (f32[4,24,3584]{2,1,0:T(8,128)S(1)}, f32[4,24,3584]{2,1,0:T(8,128)}, u32[]{:S(2)}) copy-start(f32[4,24,3584]{2,1,0:T(8,128)} %convert_reduce_fusion) | copy-start | bytes 4128772
  293.4 63.7 %copy-start.3 = (bf16[64,3584]{1,0:T(8,128)(2,1)S(1)}, bf16[64,3584]{1,0:T(8,128)(2,1)}, u32[]{:S(2)}) copy-start(bf16[64,3584]{1,0:T(8,128)(2,1)} %copy-done.2) | copy-start | bytes 1376260
  293.4 65.5 %copy-start.5 = (bf16[64,3584]{1,0:T(8,128)(2,1)S(1)}, bf16[64,3584]{1,0:T(8,128)(2,1)}, u32[]{:S(2)}) copy-start(bf16[64,3584]{1,0:T(8,128)(2,1)} %copy-done.4) | copy-start | bytes 1376260
where the time goes:
time: 363 us; the launch traced here: 361 us
  waiting for transfers between devices  261 us (72%)
  matrix products  46.2 us (13%)
  starting transfers between devices  35.6 us (10%)
  local copies, waits for them, and re-layouts  9.11 us (3%)
  other arithmetic  8.24 us (2%)
    all_to_all x1, waiting for transfers between devices, local(): lax.all_to_all(forward_part, 'expert', split_axis=0, concat_axis=0, tiled...  61.3 us
    all_to_all x1, waiting for transfers between devices, local(): lax.all_to_all(backward_part, 'expert', split_axis=0, concat_axis=0, tile...  48.5 us
    all_to_all x1, waiting for transfers between devices, local(): lax.all_to_all(saved_send, 'expert', split_axis=0, concat_axis=0, tiled=T...  46 us
    all_to_all x1, waiting for transfers between devices, local(): lax.all_to_all(grad_send, 'expert', split_axis=0, concat_axis=0, tiled=True)  45.3 us
    all_to_all x1, waiting for transfers between devices, local(): lax.all_to_all(fwd_send, 'expert', split_axis=0, concat_axis=0, tiled=True)  37.2 us
    ppermute x2, waiting for transfers between devices, passed_along(): return lax.ppermute(block, axis, route)  22.7 us
    dot_general x1, matrix products, expert_backward(): lax.dot_general(grad_gate, gate_weight, contract, preferred_element_type=...  9.23 us
    dot_general x1, matrix products, expert_forward(): jnp.dot(active, down_weight, preferred_element_type=jnp.float32)  8.92 us
  transfers between devices with their start and end apart: 7, of which 7 were waited for; matrix products, arithmetic and copies ran while one was open for 13% of the time, Pallas kernels for 0%

commit v1 on v0

v1 whole, which is shorter than its diff:
```python
import functools

import jax
import jax.numpy as jnp
from jax import lax
from jax.experimental import pallas as pl
from jax.experimental.pallas import tpu as pltpu
from jax.sharding import PartitionSpec as P

D = 3584
HALF = D // 2
TOK = 64
HID = 512
MOST = 24
BLOCK = 2 * MOST
ROWS = 4 * BLOCK
TILE = 256
MESH = pl.DeviceIdType.MESH
F32 = jnp.float32
BF16 = jnp.bfloat16
NN = (((1,), (0,)), ((), ()))
NT = (((1,), (1,)), ((), ()))

N_SEM = 128


def dot(a, b, how=NN):
    return lax.dot_general(a, b, how, preferred_element_type=F32)


def kernel(
    acts,
    f_route,
    f_gate,
    saved,
    grads,
    b_route,
    b_gate,
    w_gate,
    w_up,
    w_down,
    f_out,
    b_out,
    wg,
    wu,
    wd,
    meta,
    f_place,
    b_place,
    f_pick,
    b_pick,
    tok_s,
    tok_g,
    tok_f,
    pk_s,
    pk_g,
    pk_f,
    rx_s,
    rx_g,
    rx_f,
    hid_a,
    hid_b,
    b_psend,
    b_precv,
    b_own,
    b_far,
    b_pr,
    b_home,
    b_ret,
    f_psend,
    f_precv,
    f_own,
    f_far,
    f_pr,
    f_home,
    f_ret,
    outs_send,
    outs_recv,
    send_sem,
    recv_sem,
    load_sem,
):
    sec = lax.axis_index("pipe")
    ex = lax.axis_index("expert")
    n_sec = lax.axis_size("pipe")
    n_ex = lax.axis_size("expert")
    z = lax.div(ex, 2)
    c = lax.rem(ex, 2)
    sgn = 1 - 2 * lax.rem(z, 2)
    pair = lax.div(z, 2)

    def along(dist):
        return (sec, lax.rem(ex + 2 * dist * sgn + 2 * n_ex, n_ex))

    other = (sec, ex + 1 - 2 * c)
    partner = along(1)
    target = {1: along(-1), 2: along(2), 3: along(-3)}
    source = {1: along(-1), 2: along(-2), 3: along(-3)}
    nxt = lax.rem(sec + 1, n_sec)
    prv = lax.rem(sec + n_sec - 1, n_sec)

    count = [0]
    pending = []

    def copy(src, dst, to, sem=None):
        i = count[0]
        count[0] += 1
        out = pltpu.make_async_remote_copy(
            src_ref=src,
            dst_ref=dst,
            send_sem=send_sem.at[i],
            recv_sem=recv_sem.at[i] if sem is None else recv_sem.at[sem],
            device_id=to,
            device_id_type=MESH,
        )
        pending.append(out)
        return out

    loads = [
        pltpu.make_async_copy(w_gate.at[0], wg, load_sem.at[0]),
        pltpu.make_async_copy(w_up.at[0], wu, load_sem.at[1]),
        pltpu.make_async_copy(w_down.at[0], wd, load_sem.at[2]),
    ]
    mine = pl.ds(pl.multiple_of(c * TOK, TOK), TOK)
    half_mine = pl.ds(pl.multiple_of(c * HALF, HALF), HALF)
    half_other = pl.ds(pl.multiple_of((1 - c) * HALF, HALF), HALF)
    own_saved = pltpu.make_async_copy(
        saved.at[0, :, half_mine], tok_s.at[mine], load_sem.at[3]
    )
    own_saved.start()

    barrier = pltpu.get_barrier_semaphore()
    friends = [
        other,
        partner,
        along(-1),
        along(2),
        along(-2),
        along(-3),
        (nxt, 2 * z),
        (nxt, 2 * z + 1),
        (prv, 2 * z),
        (prv, 2 * z + 1),
    ]
    for friend in friends:
        pl.semaphore_signal(barrier, inc=1, device_id=friend, device_id_type=MESH)
    for load in loads:
        load.start()

    lane = lax.broadcasted_iota(jnp.int32, (TOK, 128), 1)
    row = lax.broadcasted_iota(jnp.int32, (TOK, TOK), 0)
    col = lax.broadcasted_iota(jnp.int32, (TOK, TOK), 1)
    below = jnp.where(col < row, 1.0, 0.0).astype(BF16)
    for which, (route, gate) in enumerate(((f_route, f_gate), (b_route, b_gate))):
        named = jnp.broadcast_to(route[0], (TOK, 128))
        turn = lax.rem((named - pair) * sgn + 8, 4)
        near = jnp.where(turn == 0, 0, jnp.where(turn == 1, 2, jnp.where(turn == 2, 3, 1)))
        hot = jnp.where(near == lane, 1.0, 0.0)
        before = dot(below, hot.astype(BF16))
        rank = jnp.sum(hot * before, axis=1, keepdims=True)
        slot = (near * BLOCK + c * MOST).astype(F32) + rank
        meta[mine, which * 128 : which * 128 + 128] = slot
        meta[mine, 256 + which * 128 : 384 + which * 128] = jnp.broadcast_to(gate[0], (TOK, 128))
    f_ret[ROWS:, :] = jnp.zeros((256 - ROWS, HALF), BF16)
    b_ret[ROWS:, :] = jnp.zeros((256 - ROWS, HALF), BF16)

    pl.semaphore_wait(barrier, len(friends))

    swap_meta = copy(meta.at[mine], meta.at[mine], other)
    swap_meta.start()
    swap_saved = copy(saved.at[0, :, half_other], tok_s.at[mine], other)
    swap_saved.start()

    def relay_pipe(tokens, land, to_sec):
        base = count[0]
        for half in range(2):
            cp = copy(
                tokens.at[0, :, half * HALF : half * HALF + HALF],
                land.at[mine],
                (to_sec, 2 * z + half),
                sem=base + c,
            )
            cp.start()

        def wait():
            for src in range(2):
                pltpu.make_async_remote_copy(
                    src_ref=tokens.at[0, :, 0:HALF],
                    dst_ref=land.at[src * TOK : src * TOK + TOK],
                    send_sem=send_sem.at[base],
                    recv_sem=recv_sem.at[base + src],
                    device_id=other,
                    device_id_type=MESH,
                ).wait_recv()

        return wait

    wait_g = relay_pipe(grads, tok_g, prv)
    wait_f = relay_pipe(acts, tok_f, nxt)

    swap_meta.wait_recv()
    lanes = lax.broadcasted_iota(jnp.int32, (2 * TOK, 128), 1).astype(F32)
    for which, (place, pick) in enumerate(((f_place, f_pick), (b_place, b_pick))):
        slot = meta[:, which * 128 : which * 128 + 128]
        hot = jnp.concatenate(
            [jnp.where(slot == lanes, 1.0, 0.0), jnp.where(slot == lanes + 128.0, 1.0, 0.0)], axis=1
        )
        pick[...] = hot.astype(BF16)
        place[...] = hot.T.astype(BF16)

    def rows(k, n=1):
        return slice(k * BLOCK, (k + n) * BLOCK)

    class Dispatch:
        def __init__(self, tok, place, pk, rx):
            self.tok, self.place, self.pk, self.rx = tok, place, pk, rx
            self.near, self.over, self.cross = {}, {}, {}

        def send(self):
            for j in range(0, HALF, TILE):
                self.pk[:, j : j + TILE] = dot(
                    self.place[0:ROWS, :], self.tok[:, j : j + TILE]
                ).astype(BF16)
            for k in (3, 2, 1):
                self.near[k] = copy(self.pk.at[rows(k)], self.rx.at[c, rows(k)], target[k])
                self.near[k].start()
            self.rx[c, rows(0)] = self.pk[rows(0)]
            self.relay(0)

        def relay(self, k):
            if k:
                self.near[k].wait_recv()
            here = self.rx.at[c, rows(k)]
            self.over[k] = copy(here, self.rx.at[c, rows(4 + k)], partner)
            self.over[k].start()
            self.cross[k] = copy(here, here, other)
            self.cross[k].start()

        def hand(self, k):
            self.over[k].wait_recv()
            here = self.rx.at[c, rows(4 + k)]
            self.cross[4 + k] = copy(here, here, other)
            self.cross[4 + k].start()

        def ready(self, ks):
            for k in ks:
                self.cross[k].wait_recv()

    ds = Dispatch(tok_s, b_place, pk_s, rx_s)
    dg = Dispatch(tok_g, b_place, pk_g, rx_g)
    df = Dispatch(tok_f, f_place, pk_f, rx_f)

    def x_of(ref, chunk):
        first = chunk * ROWS
        return ref[0, first : first + ROWS, :], ref[1, first : first + ROWS, :]

    def hidden_bwd(chunk):
        @pl.loop(0, HID // TILE)
        def _(n):
            cols = pl.ds(pl.multiple_of(n * TILE, TILE), TILE)
            x0, x1 = x_of(rx_s, chunk)
            pre = dot(x0, wg[0:HALF, cols]) + dot(x1, wg[HALF:D, cols])
            up = dot(x0, wu[0:HALF, cols]) + dot(x1, wu[HALF:D, cols])
            g0, g1 = x_of(rx_g, chunk)
            back = dot(g0, wd[cols, 0:HALF], NT) + dot(g1, wd[cols, HALF:D], NT)
            sig = lax.logistic(pre)
            hid_b[:, cols] = (back * pre * sig).astype(BF16)
            hid_a[:, cols] = (back * up * sig * (1.0 + pre * (1.0 - sig))).astype(BF16)

    def hidden_fwd(chunk):
        @pl.loop(0, HID // TILE)
        def _(n):
            cols = pl.ds(pl.multiple_of(n * TILE, TILE), TILE)
            x0, x1 = x_of(rx_f, chunk)
            pre = dot(x0, wg[0:HALF, cols]) + dot(x1, wg[HALF:D, cols])
            up = dot(x0, wu[0:HALF, cols]) + dot(x1, wu[HALF:D, cols])
            hid_a[:, cols] = (pre * lax.logistic(pre) * up).astype(BF16)

    def out_bwd(half, into):
        @pl.loop(0, HALF // TILE)
        def _(j):
            at = pl.ds(pl.multiple_of(half * HALF + j * TILE, TILE), TILE)
            got = dot(hid_a[...], wg[at, :], NT) + dot(hid_b[...], wu[at, :], NT)
            into[:, pl.ds(pl.multiple_of(j * TILE, TILE), TILE)] = got.astype(into.dtype)

    def out_fwd(half, into):
        @pl.loop(0, HALF // TILE)
        def _(j):
            at = pl.ds(pl.multiple_of(half * HALF + j * TILE, TILE), TILE)
            got = dot(hid_a[...], wd[:, at])
            into[:, pl.ds(pl.multiple_of(j * TILE, TILE), TILE)] = got.astype(into.dtype)

    class Return:
        def __init__(self, hidden, out, psend, precv, own, far, pr, home, ret, pick, tok, which, result):
            self.hidden, self.out = hidden, out
            self.psend, self.precv, self.own = psend, precv, own
            self.far, self.pr, self.home, self.ret = far, pr, home, ret
            self.pick, self.tok, self.which, self.result = pick, tok, which, result
            self.part, self.over, self.back = {}, {}, {}

        def give(self, chunk):
            self.out(1 - c, self.psend.at[chunk])
            self.part[chunk] = copy(self.psend.at[chunk], self.precv.at[chunk], other)
            self.part[chunk].start()

        def keep(self, chunk):
            self.out(c, self.own.at[chunk])

        def send_far(self):
            self.part[1].wait_recv()
            for k in (3, 2, 1, 0):
                self.far[rows(k)] = (
                    self.own[1, rows(k)] + self.precv[1, rows(k)].astype(F32)
                ).astype(BF16)
                self.over[k] = copy(self.far.at[rows(k)], self.pr.at[rows(k)], partner)
                self.over[k].start()

        def sum_near(self):
            self.part[0].wait_recv()

        def send_home(self, k):
            self.over[k].wait_recv()
            total = (
                self.own[0, rows(k)]
                + self.precv[0, rows(k)].astype(F32)
                + self.pr[rows(k)].astype(F32)
            ).astype(BF16)
            if k == 0:
                self.ret[rows(0)] = total
            else:
                self.home[rows(k)] = total
                self.back[k] = copy(self.home.at[rows(k)], self.ret.at[rows(k)], source[k])
                self.back[k].start()

        def finish(self):
            for k in (1, 2, 3):
                self.back[k].wait_recv()
            gate = meta[:, 256 + self.which * 128 : 384 + self.which * 128]
            gate = jnp.concatenate([gate, gate], axis=1)

            @pl.loop(0, HALF // TILE)
            def _(j):
                cols = pl.ds(pl.multiple_of(j * TILE, TILE), TILE)
                value = dot(self.pick[...], self.ret[:, cols])
                full = (self.tok[:, cols].astype(F32) + gate * value).astype(BF16)
                outs_send[self.which, :, cols] = full

            self.result[0, :, half_mine] = outs_send[self.which, mine, :]
            theirs = pl.ds(pl.multiple_of((1 - c) * TOK, TOK), TOK)
            self.last = copy(
                outs_send.at[self.which, theirs], outs_recv.at[self.which], other
            )
            self.last.start()

        def close(self):
            self.last.wait_recv()
            self.result[0, :, half_other] = outs_recv[self.which]

    rb = Return(
        hidden_bwd, out_bwd, b_psend, b_precv, b_own, b_far, b_pr, b_home, b_ret, b_pick, tok_g, 1, b_out
    )
    rf = Return(
        hidden_fwd, out_fwd, f_psend, f_precv, f_own, f_far, f_pr, f_home, f_ret, f_pick, tok_f, 0, f_out
    )

    own_saved.wait()
    swap_saved.wait_recv()
    ds.send()
    wait_g()
    dg.send()
    for k in (1, 2, 3):
        ds.relay(k)
    for k in (1, 2, 3):
        dg.relay(k)
    wait_f()
    df.send()
    for k in range(4):
        ds.hand(k)
    for k in range(4):
        dg.hand(k)
    for load in loads:
        load.wait()
    ds.ready(range(4, 8))
    dg.ready(range(4, 8))
    df.relay(1)
    rb.hidden(1)
    df.relay(2)
    rb.give(1)
    df.relay(3)
    rb.keep(1)
    rb.send_far()
    for k in range(4):
        df.hand(k)
    ds.ready(range(4))
    dg.ready(range(4))
    rb.hidden(0)
    rb.give(0)
    rb.keep(0)
    rb.sum_near()
    for k in (3, 2, 1, 0):
        rb.send_home(k)
    df.ready(range(4, 8))
    rf.hidden(1)
    rf.give(1)
    rf.keep(1)
    rf.send_far()
    df.ready(range(4))
    rf.hidden(0)
    rf.give(0)
    rf.keep(0)
    rf.sum_near()
    rb.finish()
    for k in (3, 2, 1, 0):
        rf.send_home(k)
    rb.close()
    rf.finish()
    rf.close()
    for cp in pending:
        cp.wait_send()


def local(*args):
    vmem = pl.BlockSpec(memory_space=pltpu.VMEM)
    hbm = pl.BlockSpec(memory_space=pl.ANY)
    tok = pltpu.VMEM((2 * TOK, HALF), BF16)
    block = pltpu.VMEM((ROWS, HALF), BF16)
    two = pltpu.VMEM((2, ROWS, HALF), BF16)
    held = pltpu.VMEM((2, 2 * ROWS, HALF), BF16)
    own = pltpu.VMEM((2, ROWS, HALF), F32)
    ret = pltpu.VMEM((256, HALF), BF16)
    stream = [two, two, own, block, block, block, ret]
    shape = jax.ShapeDtypeStruct((1, TOK, D), BF16)
    return pl.pallas_call(
        kernel,
        out_shape=(shape, shape),
        in_specs=[hbm, vmem, vmem, hbm, hbm, vmem, vmem, hbm, hbm, hbm],
        out_specs=(vmem, vmem),
        scratch_shapes=[
            pltpu.VMEM((D, HID), BF16),
            pltpu.VMEM((D, HID), BF16),
            pltpu.VMEM((HID, D), BF16),
            pltpu.VMEM((2 * TOK, 512), F32),
            pltpu.VMEM((256, 2 * TOK), BF16),
            pltpu.VMEM((256, 2 * TOK), BF16),
            pltpu.VMEM((2 * TOK, 256), BF16),
            pltpu.VMEM((2 * TOK, 256), BF16),
            tok,
            tok,
            tok,
            block,
            block,
            block,
            held,
            held,
            held,
            pltpu.VMEM((ROWS, HID), BF16),
            pltpu.VMEM((ROWS, HID), BF16),
            *stream,
            *stream,
            pltpu.VMEM((2, 2 * TOK, HALF), BF16),
            pltpu.VMEM((2, TOK, HALF), BF16),
            pltpu.SemaphoreType.DMA((N_SEM,)),
            pltpu.SemaphoreType.DMA((N_SEM,)),
            pltpu.SemaphoreType.DMA((4,)),
        ],
        compiler_params=pltpu.CompilerParams(
            collective_id=0, has_side_effects=True, vmem_limit_bytes=56 * 2**20
        ),
        cost_estimate=pl.CostEstimate(
            flops=16 * 2 * ROWS * D * HID, bytes_accessed=14 * 2**20, transcendentals=4 * ROWS * HID
        ),
    )(*args)


def solution(mesh):
    row = P("pipe", "expert", None)
    col = P("pipe", None, "expert")
    return jax.shard_map(
        local,
        mesh=mesh,
        in_specs=(row,) * 7 + (col, col, row),
        out_specs=(row, row),
        check_vma=False,
    )
```

time: 363 us -> 152 us (0.42)
  waiting for transfers between devices: 261 us -> 0 us
  Pallas kernels: 0 us -> 139 us
  matrix products: 46.2 us -> 0 us
  starting transfers between devices: 35.6 us -> 0 us
  other arithmetic: 8.24 us -> 0 us
    all_to_all x5 -> x0, waiting for transfers between devices: 238 us -> none  [the longest x1 61.3 us: local(): lax.all_to_all(forward_part, 'expert', split_axis=0, concat_axis=0, tiled...]
    pallas_call x0 -> x1, Pallas kernels: none -> 139 us  [local(): pl.pallas_call(kernel, out_shape=(shape, shape), in_specs=[hbm, vmem, vme...]
    dot_general x11 -> x0, matrix products: 46.2 us -> none  [the longest x1 9.23 us: expert_backward(): lax.dot_general(grad_gate, gate_weight, contract, preferred_element_type=...]
    all_to_all x5 -> x0, starting transfers between devices: 29.4 us -> none  [the longest x1 7.99 us: local(): lax.all_to_all(saved_send, 'expert', split_axis=0, concat_axis=0, tiled=T...]
    ppermute x2 -> x0, waiting for transfers between devices: 22.7 us -> none  [passed_along(): return lax.ppermute(block, axis, route)]
    broadcast_in_dim x3 -> x0, local copies, waits for them, and re-layouts: 7.54 us -> none  [pack_rows(): return jnp.repeat(buffer, split_count, axis=0)]
    unnamed x20 -> x6, local copies, waits for them, and re-layouts: 1.57 us -> 9.05 us
    ppermute x2 -> x0, starting transfers between devices: 6.23 us -> none  [passed_along(): return lax.ppermute(block, axis, route)]
  transfers between devices with their start and end apart: 7 -> 0, of which waited for: 7 -> 0; matrix products, arithmetic and copies ran while one was open for 13% -> 0% of each run, Pallas kernels for 0% -> 0%
where the time goes in v1:
time: 152 us; the launch traced here: 149 us
  Pallas kernels  139 us (91%)
  local copies, waits for them, and re-layouts  9.05 us (6%)
    pallas_call x1, Pallas kernels, local(): pl.pallas_call(kernel, out_shape=(shape, shape), in_specs=[hbm, vmem, vme...  139 us
    unnamed x6, local copies, waits for them, and re-layouts  9.05 us

profile of v1, /device:TPU:97, one launch (start us, length us, event | category | flops | bytes accessed | tf_op | source)
XLA Modules:
  0.0 148.8 jit_solution(8644272472532493345)
XLA Ops:
  0.6 1.4 copy.12.f_route
  2.0 1.4 copy.13.f_gate
  3.3 1.4 copy.14.b_route
  4.7 1.4 copy.15.b_gate
  6.1 139.1 %shard_map.113 = (bf16[1,64,3584]{2,1,0:T(8,128)(2,1)}, bf16[1,64,3584]{2,1,0:T(8,128)(2,1)}) custom-call(bf16[1,64,3584]{2,1,0:T(8,128)(2,1)} %acts.1, s32[1,64,1]{2,1,0:T(8,128)} %copy.12.f_route, f32[1,64,1]{2,1,0:T(8,128)} %copy.13.f_gate, bf16[1,64,3584]{2,1,0:T(8,128)(2,1)} %saved.1, bf16[1,64,3584]{2,1,0:T(8,128)(2,1)} %grads.1, ...), custom_call_target="tpu_custom_call" | custom-call | flops 11274289152 | bytes 14680064 | tf_op jit(solution)/shard_map/pallas_call | solution.py:433
  145.2 1.8 %copy.18 = bf16[1,64,3584]{2,1,0:T(8,128)(2,1)} copy(bf16[1,64,3584]{2,1,0:T(8,128)(2,1)} %get-tuple-element.4) | data formatting | bytes 917504
  147.0 1.8 %copy.19 = bf16[1,64,3584]{2,1,0:T(8,128)(2,1)} copy(bf16[1,64,3584]{2,1,0:T(8,128)(2,1)} %get-tuple-element.5) | data formatting | bytes 917504

commit v2 on v1

--- a/solution.py
+++ b/solution.py
@@ -45,6 +45,7 @@
     wu,
     wd,
     meta,
+    gates,
     f_place,
     b_place,
     f_pick,
@@ -75,7 +76,6 @@
     f_home,
     f_ret,
     outs_send,
-    outs_recv,
     send_sem,
     recv_sem,
     load_sem,
@@ -147,26 +147,28 @@
     for load in loads:
         load.start()
 
-    lane = lax.broadcasted_iota(jnp.int32, (TOK, 128), 1)
+    near_of = lax.broadcasted_iota(jnp.int32, (8, TOK), 0)
     row = lax.broadcasted_iota(jnp.int32, (TOK, TOK), 0)
     col = lax.broadcasted_iota(jnp.int32, (TOK, TOK), 1)
-    below = jnp.where(col < row, 1.0, 0.0).astype(BF16)
-    for which, (route, gate) in enumerate(((f_route, f_gate), (b_route, b_gate))):
-        named = jnp.broadcast_to(route[0], (TOK, 128))
+    above = jnp.where(row < col, 1.0, 0.0).astype(BF16)
+    lines = []
+    for route in (f_route, b_route):
+        named = jnp.broadcast_to(route[...], (8, TOK))
         turn = lax.rem((named - pair) * sgn + 8, 4)
         near = jnp.where(turn == 0, 0, jnp.where(turn == 1, 2, jnp.where(turn == 2, 3, 1)))
-        hot = jnp.where(near == lane, 1.0, 0.0)
-        before = dot(below, hot.astype(BF16))
-        rank = jnp.sum(hot * before, axis=1, keepdims=True)
-        slot = (near * BLOCK + c * MOST).astype(F32) + rank
-        meta[mine, which * 128 : which * 128 + 128] = slot
-        meta[mine, 256 + which * 128 : 384 + which * 128] = jnp.broadcast_to(gate[0], (TOK, 128))
+        hot = jnp.where(near == near_of, 1.0, 0.0)
+        before = dot(hot.astype(BF16), above)
+        rank = jnp.sum(hot * before, axis=0, keepdims=True)
+        lines.append((near[0:1] * BLOCK + c * MOST).astype(F32) + rank)
+    lines += [f_gate[...], b_gate[...]]
+    for at, line in enumerate(lines):
+        meta[c, at : at + 1, :] = jnp.concatenate([line, line], axis=1)
     f_ret[ROWS:, :] = jnp.zeros((256 - ROWS, HALF), BF16)
     b_ret[ROWS:, :] = jnp.zeros((256 - ROWS, HALF), BF16)
 
     pl.semaphore_wait(barrier, len(friends))
 
-    swap_meta = copy(meta.at[mine], meta.at[mine], other)
+    swap_meta = copy(meta.at[c], meta.at[c], other)
     swap_meta.start()
     swap_saved = copy(saved.at[0, :, half_other], tok_s.at[mine], other)
     swap_saved.start()
@@ -198,15 +200,21 @@
     wait_g = relay_pipe(grads, tok_g, prv)
     wait_f = relay_pipe(acts, tok_f, nxt)
 
-    swap_meta.wait_recv()
-    lanes = lax.broadcasted_iota(jnp.int32, (2 * TOK, 128), 1).astype(F32)
-    for which, (place, pick) in enumerate(((f_place, f_pick), (b_place, b_pick))):
-        slot = meta[:, which * 128 : which * 128 + 128]
-        hot = jnp.concatenate(
-            [jnp.where(slot == lanes, 1.0, 0.0), jnp.where(slot == lanes + 128.0, 1.0, 0.0)], axis=1
-        )
-        pick[...] = hot.astype(BF16)
-        place[...] = hot.T.astype(BF16)
+    def line_of(at):
+        left = lax.broadcasted_iota(jnp.int32, (1, 2 * TOK), 1) < TOK
+        return jnp.where(left, meta[0, at : at + 1, :], meta[1, at : at + 1, :])
+
+    def make_place(which, place):
+        slots = lax.broadcasted_iota(jnp.int32, (256, 2 * TOK), 0).astype(F32)
+        hot = jnp.where(line_of(which) == slots, 1.0, 0.0)
+        place[...] = hot.astype(BF16)
+
+    def make_pick(which, pick):
+        slots = lax.broadcasted_iota(jnp.int32, (256, 2 * TOK), 0).astype(F32)
+        pick[...] = jnp.where(line_of(which) == slots, 1.0, 0.0).T.astype(BF16)
+
+    def make_gate(which):
+        gates[which] = jnp.broadcast_to(line_of(2 + which), (2 * TOK, 2 * TOK)).T
 
     def rows(k, n=1):
         return slice(k * BLOCK, (k + n) * BLOCK)
@@ -221,11 +229,14 @@
                 self.pk[:, j : j + TILE] = dot(
                     self.place[0:ROWS, :], self.tok[:, j : j + TILE]
                 ).astype(BF16)
-            for k in (3, 2, 1):
-                self.near[k] = copy(self.pk.at[rows(k)], self.rx.at[c, rows(k)], target[k])
-                self.near[k].start()
             self.rx[c, rows(0)] = self.pk[rows(0)]
             self.relay(0)
+            for k in (1, 2):
+                self.send_near(k)
+
+        def send_near(self, k):
+            self.near[k] = copy(self.pk.at[rows(k)], self.rx.at[c, rows(k)], target[k])
+            self.near[k].start()
 
         def relay(self, k):
             if k:
@@ -335,26 +346,31 @@
         def finish(self):
             for k in (1, 2, 3):
                 self.back[k].wait_recv()
-            gate = meta[:, 256 + self.which * 128 : 384 + self.which * 128]
+            gate = gates[self.which]
             gate = jnp.concatenate([gate, gate], axis=1)
-
-            @pl.loop(0, HALF // TILE)
-            def _(j):
-                cols = pl.ds(pl.multiple_of(j * TILE, TILE), TILE)
-                value = dot(self.pick[...], self.ret[:, cols])
-                full = (self.tok[:, cols].astype(F32) + gate * value).astype(BF16)
-                outs_send[self.which, :, cols] = full
-
-            self.result[0, :, half_mine] = outs_send[self.which, mine, :]
             theirs = pl.ds(pl.multiple_of((1 - c) * TOK, TOK), TOK)
-            self.last = copy(
-                outs_send.at[self.which, theirs], outs_recv.at[self.which], other
-            )
-            self.last.start()
+            self.last = []
+            for first, last in ((0, 4), (4, 7)):
+
+                @pl.loop(first, last)
+                def _(j):
+                    cols = pl.ds(pl.multiple_of(j * TILE, TILE), TILE)
+                    value = dot(self.pick[...], self.ret[:, cols])
+                    full = (self.tok[:, cols].astype(F32) + gate * value).astype(BF16)
+                    outs_send[self.which, :, cols] = full
+
+                span = slice(first * TILE, last * TILE)
+                land = pl.ds(pl.multiple_of(c * HALF + first * TILE, TILE), (last - first) * TILE)
+                part = copy(
+                    outs_send.at[self.which, theirs, span], self.result.at[0, :, land], other
+                )
+                part.start()
+                self.last.append(part)
+                self.result[0, :, land] = outs_send[self.which, mine, span]
 
         def close(self):
-            self.last.wait_recv()
-            self.result[0, :, half_other] = outs_recv[self.which]
+            for part in self.last:
+                part.wait_recv()
 
     rb = Return(
         hidden_bwd, out_bwd, b_psend, b_precv, b_own, b_far, b_pr, b_home, b_ret, b_pick, tok_g, 1, b_out
@@ -363,55 +379,72 @@
         hidden_fwd, out_fwd, f_psend, f_precv, f_own, f_far, f_pr, f_home, f_ret, f_pick, tok_f, 0, f_out
     )
 
+    swap_meta.wait_recv()
+    make_place(1, b_place)
     own_saved.wait()
     swap_saved.wait_recv()
     ds.send()
+    make_place(0, f_place)
+    make_pick(0, f_pick)
+    make_pick(1, b_pick)
+    make_gate(0)
+    make_gate(1)
+    ds.relay(1)
+    ds.send_near(3)
     wait_g()
     dg.send()
-    for k in (1, 2, 3):
-        ds.relay(k)
-    for k in (1, 2, 3):
-        dg.relay(k)
+    dg.send_near(3)
+    ds.relay(2)
+    ds.relay(3)
+    dg.relay(1)
     wait_f()
     df.send()
+    df.send_near(3)
+    dg.relay(2)
+    dg.relay(3)
     for k in range(4):
         ds.hand(k)
-    for k in range(4):
-        dg.hand(k)
+    df.relay(1)
+    dg.hand(0)
+    df.relay(2)
+    dg.hand(1)
+    df.relay(3)
+    dg.hand(2)
+    dg.hand(3)
     for load in loads:
         load.wait()
     ds.ready(range(4, 8))
     dg.ready(range(4, 8))
-    df.relay(1)
     rb.hidden(1)
-    df.relay(2)
     rb.give(1)
-    df.relay(3)
     rb.keep(1)
     rb.send_far()
-    for k in range(4):
-        df.hand(k)
     ds.ready(range(4))
     dg.ready(range(4))
     rb.hidden(0)
+    for k in range(4):
+        df.hand(k)
     rb.give(0)
     rb.keep(0)
     rb.sum_near()
-    for k in (3, 2, 1, 0):
-        rb.send_home(k)
     df.ready(range(4, 8))
     rf.hidden(1)
+    rb.send_home(3)
     rf.give(1)
+    rb.send_home(2)
     rf.keep(1)
+    rb.send_home(1)
     rf.send_far()
+    rb.send_home(0)
     df.ready(range(4))
     rf.hidden(0)
     rf.give(0)
     rf.keep(0)
     rf.sum_near()
+    for k in (3, 2, 1):
+        rf.send_home(k)
     rb.finish()
-    for k in (3, 2, 1, 0):
-        rf.send_home(k)
+    rf.send_home(0)
     rb.close()
     rf.finish()
     rf.close()
@@ -419,7 +452,9 @@
         cp.wait_send()
 
 
-def local(*args):
+def local(acts, f_route, f_gate, saved, grads, b_route, b_gate, w_gate, w_up, w_down):
+    small = [v.reshape(1, TOK) for v in (f_route, f_gate, b_route, b_gate)]
+    args = (acts, *small[:2], saved, grads, *small[2:], w_gate, w_up, w_down)
     vmem = pl.BlockSpec(memory_space=pltpu.VMEM)
     hbm = pl.BlockSpec(memory_space=pl.ANY)
     tok = pltpu.VMEM((2 * TOK, HALF), BF16)
@@ -432,14 +467,15 @@
     shape = jax.ShapeDtypeStruct((1, TOK, D), BF16)
     return pl.pallas_call(
         kernel,
-        out_shape=(shape, shape),
+        out_shape=(pltpu.VMEM((1, TOK, D), BF16),) * 2,
         in_specs=[hbm, vmem, vmem, hbm, hbm, vmem, vmem, hbm, hbm, hbm],
         out_specs=(vmem, vmem),
         scratch_shapes=[
             pltpu.VMEM((D, HID), BF16),
             pltpu.VMEM((D, HID), BF16),
             pltpu.VMEM((HID, D), BF16),
-            pltpu.VMEM((2 * TOK, 512), F32),
+            pltpu.VMEM((2, 8, 2 * TOK), F32),
+            pltpu.VMEM((2, 2 * TOK, 2 * TOK), F32),
             pltpu.VMEM((256, 2 * TOK), BF16),
             pltpu.VMEM((256, 2 * TOK), BF16),
             pltpu.VMEM((2 * TOK, 256), BF16),
@@ -458,7 +494,6 @@
             *stream,
             *stream,
             pltpu.VMEM((2, 2 * TOK, HALF), BF16),
-            pltpu.VMEM((2, TOK, HALF), BF16),
             pltpu.SemaphoreType.DMA((N_SEM,)),
             pltpu.SemaphoreType.DMA((N_SEM,)),
             pltpu.SemaphoreType.DMA((4,)),

time: 152 us -> 134 us (0.88); the launches traced: 149 us -> 133 us
  Pallas kernels: 139 us -> 131 us
  local copies, waits for them, and re-layouts: 9.05 us -> 1.54 us
    pallas_call x1, Pallas kernels: 139 us -> 131 us  [local(): pl.pallas_call(kernel, out_shape=(pltpu.VMEM((1, TOK, D), BF16),) * 2, in...]
    unnamed x6 -> x2, local copies, waits for them, and re-layouts: 9.05 us -> 1.54 us
where the time goes in v2:
time: 134 us; the launch traced here: 133 us
  Pallas kernels  131 us (98%)
  local copies, waits for them, and re-layouts  1.54 us (1%)
    pallas_call x1, Pallas kernels, local(): pl.pallas_call(kernel, out_shape=(pltpu.VMEM((1, TOK, D), BF16),) * 2, in...  131 us

profile of v2, /device:TPU:97, one launch (start us, length us, event | category | flops | bytes accessed | tf_op | source)
XLA Modules:
  0.0 133.1 jit_solution(12409775751846268811)
XLA Ops:
  0.6 130.9 %shard_map.113 = (bf16[1,64,3584]{2,1,0:T(8,128)(2,1)S(1)}, bf16[1,64,3584]{2,1,0:T(8,128)(2,1)S(1)}) custom-call(bf16[1,64,3584]{2,1,0:T(8,128)(2,1)} %acts.1, s32[1,64]{1,0:T(1,128)} %bitcast.4, f32[1,64]{1,0:T(1,128)} %bitcast.5, bf16[1,64,3584]{2,1,0:T(8,128)(2,1)} %saved.1, bf16[1,64,3584]{2,1,0:T(8,128)(2,1)} %grads.1, s32[1,64]{1,0:T(1,128)} %bitcast.6, ...), custom_call_target="tpu_custom_call" | custom-call | flops 11274289152 | bytes 14680064 | tf_op jit(solution)/shard_map/pallas_call | solution.py:468
  131.5 0.8 copy.14
  132.3 0.8 copy.15

commit v3 on v2

--- a/solution.py
+++ b/solution.py
@@ -22,6 +22,8 @@
 NT = (((1,), (1,)), ((), ()))
 
 N_SEM = 128
+WHOLE = (slice(0, HALF),)
+PARTS = (slice(0, 4 * TILE), slice(4 * TILE, HALF))
 
 
 def dot(a, b, how=NN):
@@ -44,7 +46,9 @@
     wg,
     wu,
     wd,
-    meta,
+    routes,
+    weights,
+    notes,
     gates,
     f_place,
     b_place,
@@ -99,6 +103,10 @@
     nxt = lax.rem(sec + 1, n_sec)
     prv = lax.rem(sec + n_sec - 1, n_sec)
 
+    def order_at(chip):
+        second, eighth = jnp.where(chip == 2, 1, 0), jnp.where(chip == 7, 1, 0)
+        return 3 - second - 2 * eighth, 2 - second, 1 + 2 * (second + eighth)
+
     count = [0]
     pending = []
 
@@ -127,7 +135,12 @@
     own_saved = pltpu.make_async_copy(
         saved.at[0, :, half_mine], tok_s.at[mine], load_sem.at[3]
     )
-    own_saved.start()
+    small = ((routes, (f_route, b_route)), (weights, (f_gate, b_gate)))
+    small_loads = []
+    for which in (1, 0):
+        for kind, (held, given) in enumerate(small):
+            at = load_sem.at[4 + 2 * which + kind]
+            small_loads.append(pltpu.make_async_copy(given[which], held.at[which], at))
 
     barrier = pltpu.get_barrier_semaphore()
     friends = [
@@ -144,34 +157,20 @@
     ]
     for friend in friends:
         pl.semaphore_signal(barrier, inc=1, device_id=friend, device_id_type=MESH)
-    for load in loads:
+    for load in (*small_loads, own_saved, *loads):
         load.start()
 
-    near_of = lax.broadcasted_iota(jnp.int32, (8, TOK), 0)
-    row = lax.broadcasted_iota(jnp.int32, (TOK, TOK), 0)
-    col = lax.broadcasted_iota(jnp.int32, (TOK, TOK), 1)
-    above = jnp.where(row < col, 1.0, 0.0).astype(BF16)
-    lines = []
-    for route in (f_route, b_route):
-        named = jnp.broadcast_to(route[...], (8, TOK))
-        turn = lax.rem((named - pair) * sgn + 8, 4)
-        near = jnp.where(turn == 0, 0, jnp.where(turn == 1, 2, jnp.where(turn == 2, 3, 1)))
-        hot = jnp.where(near == near_of, 1.0, 0.0)
-        before = dot(hot.astype(BF16), above)
-        rank = jnp.sum(hot * before, axis=0, keepdims=True)
-        lines.append((near[0:1] * BLOCK + c * MOST).astype(F32) + rank)
-    lines += [f_gate[...], b_gate[...]]
-    for at, line in enumerate(lines):
-        meta[c, at : at + 1, :] = jnp.concatenate([line, line], axis=1)
-    f_ret[ROWS:, :] = jnp.zeros((256 - ROWS, HALF), BF16)
-    b_ret[ROWS:, :] = jnp.zeros((256 - ROWS, HALF), BF16)
-
     pl.semaphore_wait(barrier, len(friends))
 
-    swap_meta = copy(meta.at[c], meta.at[c], other)
-    swap_meta.start()
     swap_saved = copy(saved.at[0, :, half_other], tok_s.at[mine], other)
     swap_saved.start()
+    for load in small_loads:
+        load.wait()
+    for which in range(2):
+        notes[c, which : which + 1, 0:TOK] = routes[which].astype(F32)
+        notes[c, 2 + which : 3 + which, 0:TOK] = weights[which]
+    swap_notes = copy(notes.at[c], notes.at[c], other)
+    swap_notes.start()
 
     def relay_pipe(tokens, land, to_sec):
         base = count[0]
@@ -200,24 +199,48 @@
     wait_g = relay_pipe(grads, tok_g, prv)
     wait_f = relay_pipe(acts, tok_f, nxt)
 
-    def line_of(at):
-        left = lax.broadcasted_iota(jnp.int32, (1, 2 * TOK), 1) < TOK
-        return jnp.where(left, meta[0, at : at + 1, :], meta[1, at : at + 1, :])
-
-    def make_place(which, place):
+    def both(at):
+        return jnp.concatenate([notes[0, at : at + 1, 0:TOK], notes[1, at : at + 1, 0:TOK]], axis=1)
+
+    def slots_of(which):
+        tokens = 2 * TOK
+        named = jnp.broadcast_to(both(which).astype(jnp.int32), (8, tokens))
+        turn = jnp.bitwise_and((named - pair) * sgn + 8, 3)
+        near = jnp.where(turn == 0, 0, jnp.where(turn == 1, 2, jnp.where(turn == 2, 3, 1)))
+        hot = jnp.where(near == lax.broadcasted_iota(jnp.int32, (8, tokens), 0), 1.0, 0.0)
+        row = lax.broadcasted_iota(jnp.int32, (tokens, tokens), 0)
+        col = lax.broadcasted_iota(jnp.int32, (tokens, tokens), 1)
+        ahead = (row < col) & ((row < TOK) == (col < TOK))
+        before = dot(hot.astype(BF16), jnp.where(ahead, 1.0, 0.0).astype(BF16))
+        rank = jnp.sum(hot * before, axis=0, keepdims=True)
+        core = jnp.where(lax.broadcasted_iota(jnp.int32, (1, tokens), 1) < TOK, 0, MOST)
+        return (near[0:1] * BLOCK + core).astype(F32) + rank
+
+    def hot_of(line):
         slots = lax.broadcasted_iota(jnp.int32, (256, 2 * TOK), 0).astype(F32)
-        hot = jnp.where(line_of(which) == slots, 1.0, 0.0)
-        place[...] = hot.astype(BF16)
-
-    def make_pick(which, pick):
-        slots = lax.broadcasted_iota(jnp.int32, (256, 2 * TOK), 0).astype(F32)
-        pick[...] = jnp.where(line_of(which) == slots, 1.0, 0.0).T.astype(BF16)
+        return jnp.where(line == slots, 1.0, 0.0)
 
     def make_gate(which):
-        gates[which] = jnp.broadcast_to(line_of(2 + which), (2 * TOK, 2 * TOK)).T
+        line = jnp.broadcast_to(both(2 + which), (2 * TOK, 2 * TOK))
+        gates[which] = line.T
 
     def rows(k, n=1):
         return slice(k * BLOCK, (k + n) * BLOCK)
+
+    def span_of(k):
+        if isinstance(k, int):
+            return rows(k)
+        return pl.ds(pl.multiple_of(k * BLOCK, BLOCK), BLOCK)
+
+    def arrival(src, dst, sem):
+        pltpu.make_async_remote_copy(
+            src_ref=src,
+            dst_ref=dst,
+            send_sem=send_sem.at[0],
+            recv_sem=recv_sem.at[sem],
+            device_id=other,
+            device_id_type=MESH,
+        ).wait_recv()
 
     class Dispatch:
         def __init__(self, tok, place, pk, rx):
@@ -302,12 +325,13 @@
             into[:, pl.ds(pl.multiple_of(j * TILE, TILE), TILE)] = got.astype(into.dtype)
 
     class Return:
-        def __init__(self, hidden, out, psend, precv, own, far, pr, home, ret, pick, tok, which, result):
+        def __init__(self, hidden, out, psend, precv, own, far, pr, home, ret, pick, tok, which, result, spans, far_order):
             self.hidden, self.out = hidden, out
             self.psend, self.precv, self.own = psend, precv, own
             self.far, self.pr, self.home, self.ret = far, pr, home, ret
             self.pick, self.tok, self.which, self.result = pick, tok, which, result
-            self.part, self.over, self.back = {}, {}, {}
+            self.part, self.over, self.back, self.last = {}, {}, {}, []
+            self.spans, self.far_order = spans, far_order
 
         def give(self, chunk):
             self.out(1 - c, self.psend.at[chunk])
@@ -319,76 +343,90 @@
 
         def send_far(self):
             self.part[1].wait_recv()
-            for k in (3, 2, 1, 0):
-                self.far[rows(k)] = (
-                    self.own[1, rows(k)] + self.precv[1, rows(k)].astype(F32)
-                ).astype(BF16)
-                self.over[k] = copy(self.far.at[rows(k)], self.pr.at[rows(k)], partner)
-                self.over[k].start()
+            for n, cols in enumerate(self.spans):
+                base = count[0]
+                for k in (*self.far_order, 0):
+                    at = span_of(k)
+                    self.far[at, cols] = (
+                        self.own[1, at, cols] + self.precv[1, at, cols].astype(F32)
+                    ).astype(BF16)
+                    copy(self.far.at[at, cols], self.pr.at[at, cols], partner, sem=base + k).start()
+                self.over[n] = base
 
         def sum_near(self):
             self.part[0].wait_recv()
 
-        def send_home(self, k):
-            self.over[k].wait_recv()
+        def send_home(self, k, n=0):
+            cols = self.spans[n]
+            at = span_of(k)
+            arrival(self.far.at[at, cols], self.pr.at[at, cols], self.over[n] + k)
             total = (
-                self.own[0, rows(k)]
-                + self.precv[0, rows(k)].astype(F32)
-                + self.pr[rows(k)].astype(F32)
+                self.own[0, at, cols]
+                + self.precv[0, at, cols].astype(F32)
+                + self.pr[at, cols].astype(F32)
             ).astype(BF16)
-            if k == 0:
-                self.ret[rows(0)] = total
+            if isinstance(k, int) and k == 0:
+                self.ret[at, cols] = total
             else:
-                self.home[rows(k)] = total
-                self.back[k] = copy(self.home.at[rows(k)], self.ret.at[rows(k)], source[k])
-                self.back[k].start()
-
-        def finish(self):
+                self.home[at, cols] = total
+                if n not in self.back:
+                    self.back[n] = count[0]
+                    count[0] += 3
+                copy(
+                    self.home.at[at, cols],
+                    self.ret.at[at, cols],
+                    along(-k),
+                    sem=self.back[n] + k - 1,
+                ).start()
+
+        def finish(self, n=0):
             for k in (1, 2, 3):
-                self.back[k].wait_recv()
+                at = span_of(k)
+                arrival(self.home.at[at, self.spans[n]], self.ret.at[at, self.spans[n]], self.back[n] + k - 1)
             gate = gates[self.which]
             gate = jnp.concatenate([gate, gate], axis=1)
             theirs = pl.ds(pl.multiple_of((1 - c) * TOK, TOK), TOK)
-            self.last = []
-            for first, last in ((0, 4), (4, 7)):
-
-                @pl.loop(first, last)
-                def _(j):
-                    cols = pl.ds(pl.multiple_of(j * TILE, TILE), TILE)
-                    value = dot(self.pick[...], self.ret[:, cols])
-                    full = (self.tok[:, cols].astype(F32) + gate * value).astype(BF16)
-                    outs_send[self.which, :, cols] = full
-
-                span = slice(first * TILE, last * TILE)
-                land = pl.ds(pl.multiple_of(c * HALF + first * TILE, TILE), (last - first) * TILE)
-                part = copy(
-                    outs_send.at[self.which, theirs, span], self.result.at[0, :, land], other
-                )
-                part.start()
-                self.last.append(part)
-                self.result[0, :, land] = outs_send[self.which, mine, span]
+            span = self.spans[n]
+            width = span.stop - span.start
+
+            @pl.loop(span.start // TILE, span.stop // TILE)
+            def _(j):
+                cols = pl.ds(pl.multiple_of(j * TILE, TILE), TILE)
+                value = dot(self.pick[...], self.ret[:, cols])
+                full = (self.tok[:, cols].astype(F32) + gate * value).astype(BF16)
+                outs_send[self.which, :, cols] = full
+
+            land = pl.ds(pl.multiple_of(c * HALF + span.start, TILE), width)
+            part = copy(outs_send.at[self.which, theirs, span], self.result.at[0, :, land], other)
+            part.start()
+            self.last.append(part)
+            self.result[0, :, land] = outs_send[self.which, mine, span]
 
         def close(self):
             for part in self.last:
                 part.wait_recv()
 
     rb = Return(
-        hidden_bwd, out_bwd, b_psend, b_precv, b_own, b_far, b_pr, b_home, b_ret, b_pick, tok_g, 1, b_out
+        hidden_bwd, out_bwd, b_psend, b_precv, b_own, b_far, b_pr, b_home, b_ret, b_pick, tok_g, 1, b_out, WHOLE, (3, 2, 1)
     )
     rf = Return(
-        hidden_fwd, out_fwd, f_psend, f_precv, f_own, f_far, f_pr, f_home, f_ret, f_pick, tok_f, 0, f_out
+        hidden_fwd, out_fwd, f_psend, f_precv, f_own, f_far, f_pr, f_home, f_ret, f_pick, tok_f, 0, f_out, WHOLE, order_at(z + sgn)
     )
 
-    swap_meta.wait_recv()
-    make_place(1, b_place)
+    swap_notes.wait_recv()
+    b_line = slots_of(1)
+    b_place[...] = hot_of(b_line).astype(BF16)
     own_saved.wait()
     swap_saved.wait_recv()
     ds.send()
-    make_place(0, f_place)
-    make_pick(0, f_pick)
-    make_pick(1, b_pick)
+    f_line = slots_of(0)
+    f_place[...] = hot_of(f_line).astype(BF16)
+    b_pick[...] = hot_of(b_line).T.astype(BF16)
+    f_pick[...] = hot_of(f_line).T.astype(BF16)
     make_gate(0)
     make_gate(1)
+    f_ret[ROWS:, :] = jnp.zeros((256 - ROWS, HALF), BF16)
+    b_ret[ROWS:, :] = jnp.zeros((256 - ROWS, HALF), BF16)
     ds.relay(1)
     ds.send_near(3)
     wait_g()
@@ -441,7 +479,7 @@
     rf.give(0)
     rf.keep(0)
     rf.sum_near()
-    for k in (3, 2, 1):
+    for k in order_at(z):
         rf.send_home(k)
     rb.finish()
     rf.send_home(0)
@@ -450,6 +488,17 @@
     rf.close()
     for cp in pending:
         cp.wait_send()
+
+
+def hand_on(f_in, b_in, f_res, b_res, sem):
+    moves = [
+        pltpu.make_async_copy(f_in, f_res, sem.at[0]),
+        pltpu.make_async_copy(b_in, b_res, sem.at[1]),
+    ]
+    for move in moves:
+        move.start()
+    for move in moves:
+        move.wait()
 
 
 def local(acts, f_route, f_gate, saved, grads, b_route, b_gate, w_gate, w_up, w_down):
@@ -465,15 +514,17 @@
     ret = pltpu.VMEM((256, HALF), BF16)
     stream = [two, two, own, block, block, block, ret]
     shape = jax.ShapeDtypeStruct((1, TOK, D), BF16)
-    return pl.pallas_call(
+    got = pl.pallas_call(
         kernel,
         out_shape=(pltpu.VMEM((1, TOK, D), BF16),) * 2,
-        in_specs=[hbm, vmem, vmem, hbm, hbm, vmem, vmem, hbm, hbm, hbm],
+        in_specs=[hbm] * 10,
         out_specs=(vmem, vmem),
         scratch_shapes=[
             pltpu.VMEM((D, HID), BF16),
             pltpu.VMEM((D, HID), BF16),
             pltpu.VMEM((HID, D), BF16),
+            pltpu.VMEM((2, 1, TOK), jnp.int32),
+            pltpu.VMEM((2, 1, TOK), F32),
             pltpu.VMEM((2, 8, 2 * TOK), F32),
             pltpu.VMEM((2, 2 * TOK, 2 * TOK), F32),
             pltpu.VMEM((256, 2 * TOK), BF16),
@@ -496,7 +547,7 @@
             pltpu.VMEM((2, 2 * TOK, HALF), BF16),
             pltpu.SemaphoreType.DMA((N_SEM,)),
             pltpu.SemaphoreType.DMA((N_SEM,)),
-            pltpu.SemaphoreType.DMA((4,)),
+            pltpu.SemaphoreType.DMA((8,)),
         ],
         compiler_params=pltpu.CompilerParams(
             collective_id=0, has_side_effects=True, vmem_limit_bytes=56 * 2**20
@@ -505,6 +556,13 @@
             flops=16 * 2 * ROWS * D * HID, bytes_accessed=14 * 2**20, transcendentals=4 * ROWS * HID
         ),
     )(*args)
+    return pl.pallas_call(
+        hand_on,
+        out_shape=(shape, shape),
+        in_specs=[vmem, vmem],
+        out_specs=(hbm, hbm),
+        scratch_shapes=[pltpu.SemaphoreType.DMA((2,))],
+    )(*(pltpu.with_memory_space_constraint(v, pltpu.VMEM) for v in got))
 
 
 def solution(mesh):

time: 134 us -> 132 us (0.985)
  local copies, waits for them, and re-layouts: 1.54 us -> 0 us
    unnamed x2 -> x0, local copies, waits for them, and re-layouts: 1.54 us -> none
where the time goes in v3:
time: 132 us
  Pallas kernels  131 us (99%)
    pallas_call x1, Pallas kernels, local(): pl.pallas_call(kernel, out_shape=(pltpu.VMEM((1, TOK, D), BF16),) * 2, in...  131 us

profile of v3, /device:TPU:97, one launch (start us, length us, event | category | flops | bytes accessed | tf_op | source)
XLA Modules:
  0.0 132.1 jit_solution(15498445503232871620)
XLA Ops:
  0.6 130.5 %shard_map.113 = (bf16[1,64,3584]{2,1,0:T(8,128)(2,1)S(1)}, bf16[1,64,3584]{2,1,0:T(8,128)(2,1)S(1)}) custom-call(bf16[1,64,3584]{2,1,0:T(8,128)(2,1)} %acts.1, s32[1,64]{1,0:T(1,128)} %bitcast.4, f32[1,64]{1,0:T(1,128)} %bitcast.5, bf16[1,64,3584]{2,1,0:T(8,128)(2,1)} %saved.1, bf16[1,64,3584]{2,1,0:T(8,128)(2,1)} %grads.1, s32[1,64]{1,0:T(1,128)} %bitcast.6, ...), custom_call_target="tpu_custom_call" | custom-call | flops 11274289152 | bytes 14680064 | tf_op jit(solution)/shard_map/pallas_call | solution.py:517
  131.2 0.9 shard_map.114

commit v4 on v3

--- a/solution.py
+++ b/solution.py
@@ -83,6 +83,7 @@
     send_sem,
     recv_sem,
     load_sem,
+    ready,
 ):
     sec = lax.axis_index("pipe")
     ex = lax.axis_index("expert")
@@ -143,24 +144,40 @@
             small_loads.append(pltpu.make_async_copy(given[which], held.at[which], at))
 
     barrier = pltpu.get_barrier_semaphore()
-    friends = [
-        other,
-        partner,
-        along(-1),
-        along(2),
-        along(-2),
-        along(-3),
-        (nxt, 2 * z),
-        (nxt, 2 * z + 1),
-        (prv, 2 * z),
-        (prv, 2 * z + 1),
-    ]
-    for friend in friends:
-        pl.semaphore_signal(barrier, inc=1, device_id=friend, device_id_type=MESH)
+    for dist in (1, -1, 2, -2, -3):
+        there = along(dist)
+        pl.semaphore_signal(
+            barrier, inc=1, device_id=(there[0], there[1] - c), device_id_type=MESH
+        )
+
+    @pl.when(c == 1)
+    def _():
+        pl.semaphore_signal(barrier, inc=1, device_id=other, device_id_type=MESH)
+
+    for there in (nxt, prv):
+        pl.semaphore_signal(barrier, inc=1, device_id=(there, 2 * z + 1), device_id_type=MESH)
     for load in (*small_loads, own_saved, *loads):
         load.start()
 
-    pl.semaphore_wait(barrier, len(friends))
+    @pl.when(c == 0)
+    def _():
+        pl.semaphore_wait(barrier, 11)
+        pl.semaphore_signal(ready, inc=1, device_id=other, device_id_type=MESH)
+
+    @pl.when(c == 1)
+    def _():
+        pl.semaphore_wait(ready, 1)
+
+    def sections_ready():
+        @pl.when(c == 1)
+        def _():
+            pl.semaphore_wait(barrier, 4)
+            pl.semaphore_signal(ready, inc=1, device_id=other, device_id_type=MESH)
+
+        @pl.when(c == 0)
+        def _():
+            pl.semaphore_wait(ready, 1)
+
 
     swap_saved = copy(saved.at[0, :, half_other], tok_s.at[mine], other)
     swap_saved.start()
@@ -196,8 +213,6 @@
 
         return wait
 
-    wait_g = relay_pipe(grads, tok_g, prv)
-    wait_f = relay_pipe(acts, tok_f, nxt)
 
     def both(at):
         return jnp.concatenate([notes[0, at : at + 1, 0:TOK], notes[1, at : at + 1, 0:TOK]], axis=1)
@@ -419,6 +434,9 @@
     own_saved.wait()
     swap_saved.wait_recv()
     ds.send()
+    sections_ready()
+    wait_g = relay_pipe(grads, tok_g, prv)
+    wait_f = relay_pipe(acts, tok_f, nxt)
     f_line = slots_of(0)
     f_place[...] = hot_of(f_line).astype(BF16)
     b_pick[...] = hot_of(b_line).T.astype(BF16)
@@ -548,6 +566,7 @@
             pltpu.SemaphoreType.DMA((N_SEM,)),
             pltpu.SemaphoreType.DMA((N_SEM,)),
             pltpu.SemaphoreType.DMA((8,)),
+            pltpu.SemaphoreType.REGULAR,
         ],
         compiler_params=pltpu.CompilerParams(
             collective_id=0, has_side_effects=True, vmem_limit_bytes=56 * 2**20

time: 132 us -> 129 us (0.977)
  the two profiles are of different devices: /device:TPU:97 before, /device:TPU:93 now
where the time goes in v4:
time: 129 us
  Pallas kernels  129 us (100%)
    pallas_call x1, Pallas kernels, local(): pl.pallas_call(kernel, out_shape=(pltpu.VMEM((1, TOK, D), BF16),) * 2, in...  128 us

profile of v4, /device:TPU:93, one launch (start us, length us, event | category | flops | bytes accessed | tf_op | source)
XLA Modules:
  0.0 129.4 jit_solution(11062652838147664676)
XLA Ops:
  0.6 127.8 %shard_map.113 = (bf16[1,64,3584]{2,1,0:T(8,128)(2,1)S(1)}, bf16[1,64,3584]{2,1,0:T(8,128)(2,1)S(1)}) custom-call(bf16[1,64,3584]{2,1,0:T(8,128)(2,1)} %acts.1, s32[1,64]{1,0:T(1,128)} %bitcast.4, f32[1,64]{1,0:T(1,128)} %bitcast.5, bf16[1,64,3584]{2,1,0:T(8,128)(2,1)} %saved.1, bf16[1,64,3584]{2,1,0:T(8,128)(2,1)} %grads.1, s32[1,64]{1,0:T(1,128)} %bitcast.6, ...), custom_call_target="tpu_custom_call" | custom-call | flops 11274289152 | bytes 14680064 | tf_op jit(solution)/shard_map/pallas_call | solution.py:535
  128.4 0.9 shard_map.114

commit v5 on v4

--- a/solution.py
+++ b/solution.py
@@ -489,8 +489,9 @@
     rf.give(1)
     rb.send_home(2)
     rf.keep(1)
+    early = len(pending)
+    rf.send_far()
     rb.send_home(1)
-    rf.send_far()
     rb.send_home(0)
     df.ready(range(4))
     rf.hidden(0)
@@ -500,11 +501,13 @@
     for k in order_at(z):
         rf.send_home(k)
     rb.finish()
+    for cp in pending[:early]:
+        cp.wait_send()
     rf.send_home(0)
     rb.close()
     rf.finish()
     rf.close()
-    for cp in pending:
+    for cp in pending[early:]:
         cp.wait_send()
 
 

time: 129 us -> 129 us (level)
  the two profiles are of different devices: /device:TPU:93 before, /device:TPU:97 now
where the time goes in v5:
time: 129 us; the launch traced here: 127 us
  Pallas kernels  127 us (98%)
    pallas_call x1, Pallas kernels, local(): pl.pallas_call(kernel, out_shape=(pltpu.VMEM((1, TOK, D), BF16),) * 2, in...  126 us

profile of v5, /device:TPU:97, one launch (start us, length us, event | category | flops | bytes accessed | tf_op | source)
XLA Modules:
  0.0 127.2 jit_solution(13532810399912351906)
XLA Ops:
  0.6 125.6 %shard_map.113 = (bf16[1,64,3584]{2,1,0:T(8,128)(2,1)S(1)}, bf16[1,64,3584]{2,1,0:T(8,128)(2,1)S(1)}) custom-call(bf16[1,64,3584]{2,1,0:T(8,128)(2,1)} %acts.1, s32[1,64]{1,0:T(1,128)} %bitcast.4, f32[1,64]{1,0:T(1,128)} %bitcast.5, bf16[1,64,3584]{2,1,0:T(8,128)(2,1)} %saved.1, bf16[1,64,3584]{2,1,0:T(8,128)(2,1)} %grads.1, s32[1,64]{1,0:T(1,128)} %bitcast.6, ...), custom_call_target="tpu_custom_call" | custom-call | flops 11274289152 | bytes 14680064 | tf_op jit(solution)/shard_map/pallas_call | solution.py:538
  126.2 0.9 shard_map.114
